TPU v7x, 32 devices: a whole 2x2x4 slice. The times are simulated.
32 devices in a mesh: groups: 2 (over y), expert: 4 (over z), dp: 2 (over x), sub: 2 (over core).
Axes of the slice: x: 2, y: 2, z: 4, core: 2. Of those that a mesh axis runs over, the one named last changes fastest.
Arguments:
- tokens: bfloat16 [8192, 1024], P(('groups', 'expert', 'dp', 'sub')), parts along dimension 0, may hold values from -6 to 6
- upstream: bfloat16 [8192, 1024], P(('groups', 'expert', 'dp', 'sub')), parts along dimension 0, may hold values from -6 to 6
- routes: int32 [8192, 2], P(('groups', 'expert', 'dp', 'sub')), parts along dimension 0, may hold values from 0 to 3, all different within a row; in each aligned block of 256 rows (0 to 255, 256 to 511, ...) at most 192 rows name the same one
- gates: float32 [8192, 2], P(('groups', 'expert', 'dp', 'sub')), parts along dimension 0, may hold values from 0.1 to 1
- w_gate: bfloat16 [4, 1024, 512], P('expert', 'sub'), may hold values from -0.1875 to 0.1875
- w_up: bfloat16 [4, 1024, 512], P('expert', 'sub'), may hold values from -0.1875 to 0.1875
- w_down: bfloat16 [4, 512, 1024], P('expert', None, 'sub'), may hold values from -0.25 to 0.25
Outputs:
- tokens_grad: bfloat16 [8192, 1024], P(('groups', 'expert', 'dp', 'sub')), parts along dimension 0
- grad_gate: float32 [8, 1024, 512], P(('groups', 'expert'), ('dp', 'sub')), parts along dimension 0
- grad_up: float32 [8, 1024, 512], P(('groups', 'expert'), ('dp', 'sub')), parts along dimension 0
- grad_down: float32 [8, 512, 1024], P(('groups', 'expert'), ('dp', 'sub')), parts along dimension 0
There are 2 independent parts, one for each index of `groups`. A program takes and returns all parts, laid end to end along the dimension named above; an argument that names none is the same for every part. Nothing has to cross between parts.
Inputs may be any that keep to these rules, and one draw needn't show every extreme that they name: `routes`: each row names 2 different experts; among the rows of one device no expert is named more than 192 times, and in some device some expert is named exactly 192 times; every expert is named somewhere.
All inputs are finite; a program needn't handle non-finite values.
Results may differ from a plain program's by a relative error of at most 0.0085.
Values may be sent and summed in bfloat16 or wider, within the bound.
A program may use at most 64 MiB of HBM per device.

v0:
```python
import jax
import jax.numpy as jnp
from jax import lax
from jax.sharding import PartitionSpec as P

TOP = 2


def contract(left, right, left_dim, right_dim):
    return lax.dot_general(
        left, right, (((left_dim,), (right_dim,)), ((), ())), preferred_element_type=jnp.float32
    )


def expert_backward(gate_pre, up_pre, rows_grad, gate_mat, up_mat, down_mat):
    sigmoid_gate = jax.nn.sigmoid(gate_pre)
    silu_gate = gate_pre * sigmoid_gate
    hidden = (silu_gate * up_pre).astype(jnp.bfloat16)
    hidden_grad = contract(rows_grad, down_mat, 1, 1)
    gate_grad = (
        hidden_grad * up_pre * sigmoid_gate * (1.0 + gate_pre * (1.0 - sigmoid_gate))
    ).astype(jnp.bfloat16)
    up_grad = (hidden_grad * silu_gate).astype(jnp.bfloat16)
    input_grad = (contract(gate_grad, gate_mat, 1, 1) + contract(up_grad, up_mat, 1, 1)).astype(
        jnp.bfloat16
    )
    return (hidden, gate_grad, up_grad, input_grad)


def per_device(tokens, upstream, routes, gates, w_gate, w_up, w_down):
    tok_rows, width = tokens.shape
    experts = lax.axis_size("expert") * w_gate.shape[0]
    capacity = min(tok_rows, 3 * tok_rows * TOP // (2 * experts))
    flat_routes = routes.reshape(-1)
    onehot = (flat_routes[:, None] == jnp.arange(experts, dtype=jnp.int32)[None, :]).astype(
        jnp.int32
    )
    position = jnp.sum((jnp.cumsum(onehot, axis=0) - 1) * onehot, axis=1)
    target = flat_routes * capacity + position
    scaled = (
        (gates[:, :, None] * upstream[:, None, :].astype(jnp.float32))
        .astype(jnp.bfloat16)
        .reshape(-1, width)
    )
    repeated = jnp.repeat(tokens, TOP, axis=0)
    empty_rows = jnp.zeros((experts * capacity, width), jnp.bfloat16)
    send_inputs = empty_rows.at[target].set(repeated).reshape(experts, capacity, width)
    send_grads = empty_rows.at[target].set(scaled).reshape(experts, capacity, width)
    whole = (
        lax.all_gather(w_gate, "sub", axis=1, tiled=True),
        lax.all_gather(w_up, "sub", axis=1, tiled=True),
        lax.all_gather(w_down, "sub", axis=2, tiled=True),
    )
    gate_mat, up_mat, down_mat = (whole[0][0], whole[1][0], whole[2][0])
    got_inputs, got_grads = (
        lax.all_to_all(send_inputs, "expert", split_axis=0, concat_axis=0, tiled=True),
        lax.all_to_all(send_grads, "expert", split_axis=0, concat_axis=0, tiled=True),
    )
    rows_in = got_inputs.reshape(-1, width)
    gate_pre = jnp.dot(rows_in, gate_mat, preferred_element_type=jnp.float32)
    up_pre = jnp.dot(rows_in, up_mat, preferred_element_type=jnp.float32)
    rows_grad = got_grads.reshape(-1, width)
    hidden, gate_grad, up_grad, input_grad = expert_backward(
        gate_pre, up_pre, rows_grad, gate_mat, up_mat, down_mat
    )
    returned = lax.all_to_all(
        input_grad.reshape(experts, capacity, width),
        "expert",
        split_axis=0,
        concat_axis=0,
        tiled=True,
    )
    picked = returned.reshape(-1, width)[target].reshape(tok_rows, TOP, width)
    tokens_grad = jnp.sum(picked.astype(jnp.float32), axis=1).astype(jnp.bfloat16)
    part_gate = contract(rows_in, gate_grad, 0, 0)
    part_up = contract(rows_in, up_grad, 0, 0)
    part_down = contract(hidden, rows_grad, 0, 0)
    summed = (
        lax.psum(part_gate.astype(jnp.bfloat16), ("dp", "sub")).astype(jnp.float32),
        lax.psum(part_up.astype(jnp.bfloat16), ("dp", "sub")).astype(jnp.float32),
        lax.psum(part_down.astype(jnp.bfloat16), ("dp", "sub")).astype(jnp.float32),
    )
    pieces = lax.axis_size(("dp", "sub"))
    member = lax.axis_index(("dp", "sub"))
    slices = [
        lax.dynamic_slice_in_dim(
            matrix, member * (matrix.shape[0] // pieces), matrix.shape[0] // pieces, 0
        )
        for matrix in summed
    ]
    return (tokens_grad, slices[0][None], slices[1][None], slices[2][None])


def solution(mesh):
    in_specs = (
        P(("groups", "expert", "dp", "sub"), None),
        P(("groups", "expert", "dp", "sub"), None),
        P(("groups", "expert", "dp", "sub"), None),
        P(("groups", "expert", "dp", "sub"), None),
        P("expert", "sub", None),
        P("expert", "sub", None),
        P("expert", None, "sub"),
    )
    out_specs = (
        P(("groups", "expert", "dp", "sub"), None),
        P(("groups", "expert"), ("dp", "sub"), None),
        P(("groups", "expert"), ("dp", "sub"), None),
        P(("groups", "expert"), ("dp", "sub"), None),
    )
    return jax.shard_map(
        per_device, mesh=mesh, in_specs=in_specs, out_specs=out_specs, check_vma=False
    )
```

profile of v0, /device:TPU:0, one launch (start us, length us, event | category | flops | bytes accessed | tf_op | source)
XLA Modules:
  0.0 207.2 jit_solution(5643554682857402084)
XLA Ops:
  7.2 0.8 copy.12
  8.0 0.1 eq.29
  8.1 0.1 eq.25
  8.3 0.7 broadcast_multiply_fusion
  9.0 1.2 reduce-window.6
  10.2 0.2 slice_reduce_fusion
  10.4 0.2 reduce-window.9
  10.6 0.1 add_bitcast_fusion
  10.6 0.1 copy.11
  10.8 0.1 mul.70
  10.9 1.6 broadcast_in_dim.22
  12.5 0.4 reshape.116
  13.0 3.8 %scatter_custom_fusion.1 = bf16[768,1024]{1,0:T(8,128)(2,1)} fusion(s32[512]{0:T(512)S(1)} %bitcast.58, bf16[512,1024]{1,0:T(8,128)(2,1)S(1)} %reshape.116, bf16[]{:T(256)} %constant.12.clone.1), kind=kCustom, calls=%fused_computation.24 | custom fusion | bytes 1572866 | tf_op jit(solution)/shard_map/scatter | solution.py:47
  16.8 0.0 copy-start.3
  16.8 6.4 %all-to-all-start.1 = ((bf16[4,192,1024]{2,1,0:T(8,128)(2,1)}), bf16[4,192,1024]{2,1,0:T(8,128)(2,1)}, u32[]{:S(2)}, u32[]{:S(2)}) async-start(bf16[4,192,1024]{2,1,0:T(8,128)(2,1)} %bitcast.6), calls=%async_computation.1 | async-start | bytes 3145728 | tf_op jit(solution)/shard_map/all_to_all | solution.py:56
  23.3 0.0 all-gather.8.cloned.1.call-start
  23.3 0.7 all-gather.8.cloned.1.call-update
  24.0 0.0 copy-done.3
  24.0 1.9 mul.74
  25.9 0.0 copy-start.4
  25.9 2.7 %mul.75 = f32[512,1024]{1,0:T(8,128)S(1)} reshape(f32[256,2,1024]{2,1,0:T(2,128)} %mul.74) | data formatting | bytes 4194304 | tf_op jit(solution)/shard_map/mul | solution.py:41
  28.6 0.0 copy-done.4
  28.6 0.1 copy.14
  28.8 0.1 mul.72
  28.9 4.0 %scatter_custom_fusion = bf16[768,1024]{1,0:T(8,128)(2,1)} fusion(s32[512]{0:T(512)S(1)} %bitcast.59, f32[512,1024]{1,0:T(8,128)S(1)} %mul.75, f32[512]{0:T(512)S(1)} %mul.72, bf16[]{:T(256)} %constant.12.clone.1), kind=kCustom, calls=%fused_computation.13 | custom fusion | flops 1048576 | bytes 3672066 | tf_op jit(solution)/shard_map/scatter | solution.py:48
  32.9 27.5 %all-to-all-done.1 = bf16[4,192,1024]{2,1,0:T(8,128)(2,1)} async-done(((bf16[4,192,1024]{2,1,0:T(8,128)(2,1)}), bf16[4,192,1024]{2,1,0:T(8,128)(2,1)}, u32[]{:S(2)}, u32[]{:S(2)}) %all-to-all-start.1) | async-done | bytes 1572896 | tf_op jit(solution)/shard_map/all_to_all | solution.py:56
  60.4 3.6 %all-to-all-start = ((bf16[4,192,1024]{2,1,0:T(8,128)(2,1)}), bf16[4,192,1024]{2,1,0:T(8,128)(2,1)S(1)}, u32[]{:S(2)}, u32[]{:S(2)}) async-start(bf16[4,192,1024]{2,1,0:T(8,128)(2,1)} %bitcast.55), calls=%async_computation | async-start | bytes 3145728 | tf_op jit(solution)/shard_map/all_to_all | solution.py:57
  63.9 0.0 all-gather.6.cloned.1.call-start
  64.0 0.7 all-gather.6.cloned.1.call-update
  64.7 0.2 all-gather.4.cloned.1.call-start
  64.9 0.5 all-gather.4.cloned.1.call-update
  65.4 0.0 all-gather.8.cloned.1.call-done
  65.4 2.7 %fusion.4 = f32[768,512]{1,0:T(8,128)S(1)} fusion(bf16[768,1024]{1,0:T(8,128)(2,1)} %bitcast.7, bf16[1,1024,512]{2,1,0:T(8,128)(2,1)} %all-gather.8.cloned.1.call-done), kind=kOutput, calls=%fused_computation.16 | convolution fusion | flops 805306368 | bytes 4194304 | tf_op jit(solution)/shard_map/dot_general | solution.py:60
  68.1 0.0 copy-start.5
  68.1 8.7 %all-gather.6.cloned.1.call-done = bf16[1,1024,512]{2,1,0:T(8,128)(2,1)} async-done(((bf16[1,512,512]{2,1,0:T(8,128)(2,1)}), bf16[1,1024,512]{2,1,0:T(8,128)(2,1)}) %all-gather.6.cloned.1.call-update) | async-done | bytes 1048592 | tf_op jit(solution)/shard_map/all_gather | solution.py:51
  76.8 3.8 %fusion.7 = f32[768,512]{1,0:T(8,128)} fusion(bf16[768,1024]{1,0:T(8,128)(2,1)} %bitcast.7, bf16[1,1024,512]{2,1,0:T(8,128)(2,1)} %all-gather.6.cloned.1.call-done), kind=kOutput, calls=%fused_computation.19 | convolution fusion | flops 805306368 | bytes 4194304 | tf_op jit(solution)/shard_map/dot_general | solution.py:61
  80.7 7.9 %all-gather.4.cloned.1.call-done = bf16[1,512,1024]{2,1,0:T(8,128)(2,1)} async-done(((bf16[1,512,512]{2,1,0:T(8,128)(2,1)}), bf16[1,512,1024]{2,1,0:T(8,128)(2,1)}) %all-gather.4.cloned.1.call-update) | async-done | bytes 1048592 | tf_op jit(solution)/shard_map/all_gather | solution.py:52
  88.6 11.8 %all-to-all-done = bf16[4,192,1024]{2,1,0:T(8,128)(2,1)S(1)} async-done(((bf16[4,192,1024]{2,1,0:T(8,128)(2,1)}), bf16[4,192,1024]{2,1,0:T(8,128)(2,1)S(1)}, u32[]{:S(2)}, u32[]{:S(2)}) %all-to-all-start) | async-done | bytes 1572896 | tf_op jit(solution)/shard_map/all_to_all | solution.py:57
  100.4 0.0 copy-done.5
  100.4 3.2 %multiply_convert_fusion.2 = (bf16[768,512]{1,0:T(8,128)(2,1)S(1)}, bf16[768,512]{1,0:T(8,128)(2,1)S(1)}) fusion(f32[768,512]{1,0:T(8,128)S(1)} %fusion.4, f32[768,512]{1,0:T(8,128)} %fusion.7, bf16[768,1024]{1,0:T(8,128)(2,1)S(1)} %bitcast.56, bf16[1,512,1024]{2,1,0:T(8,128)(2,1)} %all-gather.4.cloned.1.call-done), kind=kOutput, calls=%fused_computation.6 | convolution fusion | flops 810418176 | bytes 7340032 | tf_op jit(solution)/shard_map/dot_general | solution.py:10
  103.6 0.0 copy-start.2
  103.6 0.0 copy-start
  103.6 3.7 %convolution_convert_fusion.1 = bf16[1024,512]{1,0:T(8,128)(2,1)} fusion(bf16[768,1024]{1,0:T(8,128)(2,1)} %bitcast.7, bf16[768,512]{1,0:T(8,128)(2,1)S(1)} %get-tuple-element.7), kind=kOutput, calls=%fused_computation.11 | convolution fusion | flops 805830656 | bytes 3407872 | tf_op jit(solution)/shard_map/dot_general | solution.py:10
  107.3 0.0 copy-done.2
  107.3 0.0 copy-done
  107.3 1.0 fusion.2
  108.3 0.2 copy-done.1
  108.5 2.2 %add_convert_fusion = bf16[768,1024]{1,0:T(8,128)(2,1)} fusion(f32[768,1024]{1,0:T(8,128)S(1)} %fusion.2, bf16[768,512]{1,0:T(8,128)(2,1)S(1)} %get-tuple-element.7, bf16[1,1024,512]{2,1,0:T(8,128)(2,1)S(1)} %copy-done.1), kind=kOutput, calls=%fused_computation.3 | convolution fusion | flops 806879232 | bytes 6553600 | tf_op jit(solution)/shard_map/dot_general | solution.py:10
  110.7 3.6 %all-to-all-start.2 = ((bf16[4,192,1024]{2,1,0:T(8,128)(2,1)}), bf16[4,192,1024]{2,1,0:T(8,128)(2,1)S(1)}, u32[]{:S(2)}, u32[]{:S(2)}) async-start(bf16[4,192,1024]{2,1,0:T(8,128)(2,1)} %bitcast.10), calls=%async_computation.2 | async-start | bytes 3145728 | tf_op jit(solution)/shard_map/all_to_all | solution.py:66
  114.3 0.0 all-reduce.3.cloned.1.call-start
  114.3 0.0 copy-start.6
  114.3 0.0 copy-start.7
  114.3 3.8 %convolution_convert_fusion.2 = bf16[1024,512]{1,0:T(8,128)(2,1)} fusion(bf16[768,1024]{1,0:T(8,128)(2,1)} %bitcast.7, bf16[768,512]{1,0:T(8,128)(2,1)} %copy-done.2), kind=kOutput, calls=%fused_computation.12 | convolution fusion | flops 805830656 | bytes 3407872 | tf_op jit(solution)/shard_map/dot_general | solution.py:10
  118.1 0.0 copy-done.6
  118.1 0.0 copy-done.7
  118.1 2.1 %convolution_convert_fusion = bf16[512,1024]{1,0:T(8,128)(2,1)} fusion(bf16[768,1024]{1,0:T(8,128)(2,1)S(1)} %bitcast.57, f32[768,512]{1,0:T(8,128)S(1)} %copy-done.7, f32[768,512]{1,0:T(8,128)S(1)} %copy-done.6), kind=kOutput, calls=%fused_computation.10 | convolution fusion | flops 808189952 | bytes 5767168 | tf_op jit(solution)/shard_map/dot_general | solution.py:10
  120.3 0.0 all-reduce.3.cloned.1.call-update
  120.3 70.3 %all-reduce.3.cloned.1.call-done = (bf16[1024,512]{1,0:T(8,128)(2,1)}, bf16[1024,512]{1,0:T(8,128)(2,1)}, bf16[512,1024]{1,0:T(8,128)(2,1)}) async-done(((bf16[1024,512]{1,0:T(8,128)(2,1)}, bf16[1024,512]{1,0:T(8,128)(2,1)}, bf16[512,1024]{1,0:T(8,128)(2,1)}), (bf16[1024,512]{1,0:T(8,128)(2,1)}, bf16[1024,512]{1,0:T(8,128)(2,1)}, bf16[512,1024]{1,0:T(8,128)(2,1)})) %all-reduce.3.cloned.1.call-update) | async-done | bytes 3145744 | tf_op jit(solution)/shard_map/psum | solution.py:79
  190.6 1.8 convert_bitcast_fusion
  192.4 2.1 %convert_bitcast_fusion.1 = (f32[1,256,512]{2,1,0:T(8,128)}, f32[1,256,512]{2,1,0:T(8,128)}) fusion(bf16[1024,512]{1,0:T(8,128)(2,1)} %get-tuple-element.5, s32[]{:T(128)S(6)} %select_n.20, bf16[1024,512]{1,0:T(8,128)(2,1)} %get-tuple-element.4), kind=kLoop, calls=%fused_computation.28 | loop fusion | flops 262144 | bytes 1572868 | tf_op jit(solution)/shard_map/broadcast_in_dim | solution.py:91
  194.6 0.0 all-to-all-done.2
  194.6 2.1 gather_fusion
  196.6 0.4 reshape.95
  197.1 3.6 %reduce_sum.25 = bf16[256,1024]{1,0:T(8,128)(2,1)} reduce(bf16[256,2,1024]{2,1,0:T(2,128)(2,1)S(1)} %reshape.95, bf16[]{:T(256)} %constant.12.clone.1), dimensions={1}, to_apply=%region_5.6 | reduce | flops 262144 | bytes 1572866 | tf_op jit(solution)/shard_map/reduce_sum | solution.py:74
  (5 shorter events, 0.0 us)
Async XLA Ops:
  16.8 7.2 %copy-start.3 = (bf16[256,1024]{1,0:T(8,128)(2,1)S(1)}, bf16[256,1024]{1,0:T(8,128)(2,1)}, u32[]{:S(2)}) copy-start(bf16[256,1024]{1,0:T(8,128)(2,1)} %param.8) | copy-start | bytes 1572868
  16.8 43.5 %all-to-all-start.1 = ((bf16[4,192,1024]{2,1,0:T(8,128)(2,1)}), bf16[4,192,1024]{2,1,0:T(8,128)(2,1)}, u32[]{:S(2)}, u32[]{:S(2)}) async-start(bf16[4,192,1024]{2,1,0:T(8,128)(2,1)} %bitcast.6), calls=%async_computation.1 | async-start | bytes 3145728 | tf_op jit(solution)/shard_map/all_to_all | solution.py:56
  23.3 42.1 %all-gather.8.cloned.1.call-start = ((), (), s32[]{:S(2)}) async-start(), calls=%async_computation.5 | async-start | bytes 1572864 | tf_op jit(solution)/shard_map/all_gather | solution.py:50
  25.9 2.7 %copy-start.4 = (f32[256,2]{0,1:T(2,128)S(1)}, f32[256,2]{0,1:T(2,128)}, u32[]{:S(2)}) copy-start(f32[256,2]{0,1:T(2,128)} %param.10) | copy-start | bytes 6148
  60.4 40.0 %all-to-all-start = ((bf16[4,192,1024]{2,1,0:T(8,128)(2,1)}), bf16[4,192,1024]{2,1,0:T(8,128)(2,1)S(1)}, u32[]{:S(2)}, u32[]{:S(2)}) async-start(bf16[4,192,1024]{2,1,0:T(8,128)(2,1)} %bitcast.55), calls=%async_computation | async-start | bytes 3145728 | tf_op jit(solution)/shard_map/all_to_all | solution.py:57
  63.9 12.9 %all-gather.6.cloned.1.call-start = ((), (), s32[]{:S(2)}) async-start(), calls=%async_computation.4 | async-start | bytes 1572864 | tf_op jit(solution)/shard_map/all_gather | solution.py:51
  64.7 23.9 %all-gather.4.cloned.1.call-start = ((), (), s32[]{:S(2)}) async-start(), calls=%async_computation.3 | async-start | bytes 1572864 | tf_op jit(solution)/shard_map/all_gather | solution.py:52
  68.1 32.2 %copy-start.5 = (f32[768,512]{1,0:T(8,128)}, f32[768,512]{1,0:T(8,128)S(1)}, u32[]{:S(2)}) copy-start(f32[768,512]{1,0:T(8,128)S(1)} %fusion.4) | copy-start | bytes 4718596
  103.6 3.7 %copy-start.2 = (bf16[768,512]{1,0:T(8,128)(2,1)}, bf16[768,512]{1,0:T(8,128)(2,1)S(1)}, u32[]{:S(2)}) copy-start(bf16[768,512]{1,0:T(8,128)(2,1)S(1)} %get-tuple-element.8) | copy-start | bytes 2359300
  103.6 3.7 %copy-start = (bf16[1,1024,512]{2,1,0:T(8,128)(2,1)S(1)}, bf16[1,1024,512]{2,1,0:T(8,128)(2,1)}, u32[]{:S(2)}) copy-start(bf16[1,1024,512]{2,1,0:T(8,128)(2,1)} %all-gather.8.cloned.1.call-done) | copy-start | bytes 3145732
  107.3 1.2 copy-start.1
  110.7 83.9 %all-to-all-start.2 = ((bf16[4,192,1024]{2,1,0:T(8,128)(2,1)}), bf16[4,192,1024]{2,1,0:T(8,128)(2,1)S(1)}, u32[]{:S(2)}, u32[]{:S(2)}) async-start(bf16[4,192,1024]{2,1,0:T(8,128)(2,1)} %bitcast.10), calls=%async_computation.2 | async-start | bytes 3145728 | tf_op jit(solution)/shard_map/all_to_all | solution.py:66
  114.3 76.4 %all-reduce.3.cloned.1.call-start = ((), (), s32[]{:S(2)}) async-start(), calls=%async_computation.6 | async-start | bytes 6291456 | tf_op jit(solution)/shard_map/psum | solution.py:79
  114.3 3.8 %copy-start.6 = (f32[768,512]{1,0:T(8,128)S(1)}, f32[768,512]{1,0:T(8,128)}, u32[]{:S(2)}) copy-start(f32[768,512]{1,0:T(8,128)} %copy-done.5) | copy-start | bytes 4718596
  114.3 3.8 %copy-start.7 = (f32[768,512]{1,0:T(8,128)S(1)}, f32[768,512]{1,0:T(8,128)}, u32[]{:S(2)}) copy-start(f32[768,512]{1,0:T(8,128)} %fusion.7) | copy-start | bytes 4718596
Sparse Core Ops, SparseCore 0:
  25.7 10.4 all-gather.7
  66.3 10.4 all-gather.5
  78.4 10.1 all-gather.3
  120.4 70.1 all-reduce.2
where the time goes:
time: 208 us; the launch traced here: 207 us
  waiting for transfers between devices  128 us (62%)
  matrix products  22.5 us (11%)
  local copies, waits for them, and re-layouts  15 us (7%)
  between operations  14 us (7%)
  starting transfers between devices  13.9 us (7%)
  other arithmetic  13.7 us (7%)
    psum x1, waiting for transfers between devices, per_device(): lax.psum(part_gate.astype(jnp.bfloat16), ('dp', 'sub')).astype(jnp.float32)  70.3 us
    all_to_all x1, waiting for transfers between devices, per_device(): lax.all_to_all(send_inputs, 'expert', split_axis=0, concat_axis=0, tiled=...  27.5 us
    dot_general x6, matrix products, contract(): lax.dot_general(left, right, (((left_dim,), (right_dim,)), ((), ())), pre...  16 us
    all_to_all x1, waiting for transfers between devices, per_device(): lax.all_to_all(send_grads, 'expert', split_axis=0, concat_axis=0, tiled=T...  11.8 us
    all_gather x1, waiting for transfers between devices, per_device(): lax.all_gather(w_up, 'sub', axis=1, tiled=True)  8.68 us
    all_gather x1, waiting for transfers between devices, per_device(): lax.all_gather(w_down, 'sub', axis=2, tiled=True)  7.94 us
    all_to_all x1, starting transfers between devices, per_device(): lax.all_to_all(send_inputs, 'expert', split_axis=0, concat_axis=0, tiled=...  6.45 us
    mul x3, local copies, waits for them, and re-layouts, per_device(): gates[:, :, None] * upstream[:, None, :].astype(jnp.float32)  4.73 us
  transfers between devices with their start and end apart: 7, of which 5 were waited for; matrix products, arithmetic and copies ran while one was open for 12% of the time, Pallas kernels for 0%

commit v1 on v0

--- a/solution.py
+++ b/solution.py
@@ -1,6 +1,10 @@
+import functools
+
 import jax
 import jax.numpy as jnp
 from jax import lax
+from jax.experimental import pallas as pl
+from jax.experimental.pallas import tpu as pltpu
 from jax.sharding import PartitionSpec as P
 
 TOP = 2
@@ -27,7 +31,7 @@
     return (hidden, gate_grad, up_grad, input_grad)
 
 
-def per_device(tokens, upstream, routes, gates, w_gate, w_up, w_down):
+def routed(tokens, upstream, routes, gates, w_gate, w_up, w_down):
     tok_rows, width = tokens.shape
     experts = lax.axis_size("expert") * w_gate.shape[0]
     capacity = min(tok_rows, 3 * tok_rows * TOP // (2 * experts))
@@ -90,6 +94,335 @@
     ]
     return (tokens_grad, slices[0][None], slices[1][None], slices[2][None])
 
+MESH = pl.DeviceIdType.MESH
+
+
+def fused_kernel(
+    n,
+    tok_ref,
+    ups_ref,
+    comb_ref,
+    wg_ref,
+    wu_ref,
+    wd_ref,
+    tg_ref,
+    gg_ref,
+    gu_ref,
+    gd_ref,
+    x_all,
+    u_all,
+    c_all,
+    w_g,
+    w_u,
+    w_d,
+    back,
+    landed,
+    acc_g,
+    acc_u,
+    acc_d,
+    sub_gu,
+    sub_d,
+    got_gu,
+    got_d,
+    dp_gu,
+    dp_d,
+    in_gu,
+    in_d,
+    ag_send,
+    ag_recv,
+    w_send,
+    w_recv,
+    ig_send,
+    ig_recv,
+    rs_send,
+    rs_recv,
+):
+    f32, bf16 = jnp.float32, jnp.bfloat16
+    group = lax.axis_index("groups")
+    z = lax.axis_index("expert")
+    d = lax.axis_index("dp")
+    s = lax.axis_index("sub")
+    rows_g = acc_g.shape[0] // 4
+    rows_d = acc_d.shape[0] // 4
+    half = w_d.shape[2]
+
+    def along(position):
+        return (group, position, d, s)
+
+    sub_peer = (group, z, d, 1 - s)
+    dp_peer = (group, z, 1 - d, s)
+
+    barrier = pltpu.get_barrier_semaphore()
+    for step in range(1, n):
+        pl.semaphore_signal(
+            barrier, inc=1, device_id=along(lax.rem(z + step, n)), device_id_type=MESH
+        )
+    pl.semaphore_signal(barrier, inc=1, device_id=sub_peer, device_id_type=MESH)
+    pl.semaphore_signal(barrier, inc=1, device_id=dp_peer, device_id_type=MESH)
+    x_all[z] = tok_ref[...]
+    u_all[z] = ups_ref[...]
+    c_all[z] = comb_ref[...]
+    w_g[s] = wg_ref[...]
+    w_u[s] = wu_ref[...]
+    w_d[s] = wd_ref[...]
+    pl.semaphore_wait(barrier, n + 1)
+
+    def copy(src, dst, send, recv, peer):
+        return pltpu.make_async_remote_copy(
+            src_ref=src,
+            dst_ref=dst,
+            send_sem=send,
+            recv_sem=recv,
+            device_id=peer,
+            device_id_type=MESH,
+        )
+
+    def block_copies(way, block):
+        target = jnp.minimum(z + 1, n - 1) if way == 0 else jnp.maximum(z - 1, 0)
+        return [
+            copy(
+                ref.at[block],
+                ref.at[block],
+                ag_send.at[way, block, i],
+                ag_recv.at[block, i],
+                along(target),
+            )
+            for i, ref in enumerate((c_all, u_all, x_all))
+        ]
+
+    can_go = (z < n - 1, z > 0)
+    for way in range(2):
+
+        @pl.when(can_go[way])
+        def _():
+            for each in block_copies(way, z):
+                each.start()
+
+    def weight_copies():
+        return [
+            copy(ref.at[s], ref.at[s], w_send.at[i], w_recv.at[i], sub_peer)
+            for i, ref in enumerate((w_g, w_u, w_d))
+        ]
+
+    def weight_waits():
+        return [
+            copy(ref.at[1 - s], ref.at[1 - s], w_send.at[i], w_recv.at[i], sub_peer)
+            for i, ref in enumerate((w_g, w_u, w_d))
+        ]
+
+    for each in weight_copies():
+        each.start()
+    acc_g[...] = jnp.zeros_like(acc_g)
+    acc_u[...] = jnp.zeros_like(acc_u)
+    acc_d[...] = jnp.zeros_like(acc_d)
+    for each in weight_waits():
+        each.wait_recv()
+
+    def back_copy(block):
+        return copy(
+            back.at[block], landed.at[z], ig_send.at[block], ig_recv.at[z], along(block)
+        )
+
+    def work(block):
+        x = x_all[block]
+        flipped = jnp.transpose(c_all[block])
+        lane = lax.broadcasted_iota(jnp.int32, flipped.shape, 1)
+        weight = jnp.sum(jnp.where(lane == z, flipped, 0.0), axis=1, keepdims=True)
+        rows_grad = (weight * u_all[block].astype(f32)).astype(bf16)
+        x_lo, x_hi = x[:, :half], x[:, half:]
+        gate_pre = contract(x_lo, w_g[0], 1, 0) + contract(x_hi, w_g[1], 1, 0)
+        up_pre = contract(x_lo, w_u[0], 1, 0) + contract(x_hi, w_u[1], 1, 0)
+        hidden_grad = contract(rows_grad[:, :half], w_d[0], 1, 1) + contract(
+            rows_grad[:, half:], w_d[1], 1, 1
+        )
+        sig = jax.nn.sigmoid(gate_pre)
+        silu = gate_pre * sig
+        hidden = (silu * up_pre).astype(bf16)
+        gate_grad = (hidden_grad * up_pre * sig * (1.0 + gate_pre * (1.0 - sig))).astype(bf16)
+        up_grad = (hidden_grad * silu).astype(bf16)
+        for j in range(2):
+            back[block, :, j * half : (j + 1) * half] = (
+                contract(gate_grad, w_g[j], 1, 1) + contract(up_grad, w_u[j], 1, 1)
+            ).astype(bf16)
+
+        @pl.when(block != z)
+        def _():
+            back_copy(block).start()
+
+        acc_g[...] += contract(x, gate_grad, 0, 0)
+        acc_u[...] += contract(x, up_grad, 0, 0)
+        acc_d[...] += contract(hidden, rows_grad, 0, 0)
+
+    def turn(i, carry):
+        step, side = i // 2, i % 2
+
+        @pl.when((side == 0) & (step > 0))
+        def _():
+            for way in range(2):
+                block = z - step if way == 0 else z + step
+                there = block >= 0 if way == 0 else block < n
+
+                @pl.when(there)
+                def _():
+                    for each in block_copies(way, block):
+                        each.wait_recv()
+
+                @pl.when(there & can_go[way])
+                def _():
+                    for each in block_copies(way, block):
+                        each.start()
+
+        block = z - step + 2 * step * side
+
+        @pl.when((block >= 0) & (block < n))
+        def _():
+            work(block)
+
+        return carry
+
+    work(z)
+    lax.fori_loop(2, 2 * n, turn, 0)
+
+    def piece_g(dd, ss):
+        return pl.ds(pl.multiple_of((dd * 2 + ss) * rows_g, rows_g), rows_g)
+
+    def piece_d(dd, ss):
+        return pl.ds(pl.multiple_of((dd * 2 + ss) * rows_d, rows_d), rows_d)
+
+    for dd in range(2):
+        sub_gu[0, dd] = acc_g[piece_g(dd, 1 - s), :].astype(bf16)
+        sub_gu[1, dd] = acc_u[piece_g(dd, 1 - s), :].astype(bf16)
+        sub_d[dd] = acc_d[piece_d(dd, 1 - s), :].astype(bf16)
+    to_sub = [
+        copy(sub_gu, got_gu, rs_send.at[0], rs_recv.at[0], sub_peer),
+        copy(sub_d, got_d, rs_send.at[1], rs_recv.at[1], sub_peer),
+    ]
+    for each in to_sub:
+        each.start()
+    for each in to_sub:
+        each.wait_recv()
+
+    def pair(acc, rows, got):
+        return acc[rows, :].astype(bf16).astype(f32) + got.astype(f32)
+
+    other = 1 - d
+    dp_gu[0] = pair(acc_g, piece_g(other, s), got_gu[0, other]).astype(bf16)
+    dp_gu[1] = pair(acc_u, piece_g(other, s), got_gu[1, other]).astype(bf16)
+    dp_d[...] = pair(acc_d, piece_d(other, s), got_d[other]).astype(bf16)
+    to_dp = [
+        copy(dp_gu, in_gu, rs_send.at[2], rs_recv.at[2], dp_peer),
+        copy(dp_d, in_d, rs_send.at[3], rs_recv.at[3], dp_peer),
+    ]
+    for each in to_dp:
+        each.start()
+    gg_ref[...] = pair(acc_g, piece_g(d, s), got_gu[0, d])
+    gu_ref[...] = pair(acc_u, piece_g(d, s), got_gu[1, d])
+    gd_ref[...] = pair(acc_d, piece_d(d, s), got_d[d])
+
+    landed[z] = back[z]
+    for source in range(n):
+
+        @pl.when(z != source)
+        def _():
+            copy(
+                back.at[source],
+                landed.at[source],
+                ig_send.at[source],
+                ig_recv.at[source],
+                along(source),
+            ).wait_recv()
+
+    total = landed[0].astype(f32)
+    for source in range(1, n):
+        total = total + landed[source].astype(f32)
+    tg_ref[...] = total.astype(bf16)
+    for each in to_dp:
+        each.wait_recv()
+    gg_ref[...] += in_gu[0].astype(f32)
+    gu_ref[...] += in_gu[1].astype(f32)
+    gd_ref[...] += in_d[...].astype(f32)
+
+    for each in to_sub + to_dp + weight_copies():
+        each.wait_send()
+    for block in range(n):
+
+        @pl.when(z != block)
+        def _():
+            back_copy(block).wait_send()
+
+        for way in range(2):
+            mine = z >= block if way == 0 else z <= block
+
+            @pl.when(mine & can_go[way])
+            def _():
+                for each in block_copies(way, block):
+                    each.wait_send()
+
+
+def fused(tokens, upstream, routes, gates, w_gate, w_up, w_down):
+    f32, bf16 = jnp.float32, jnp.bfloat16
+    rows, width = tokens.shape
+    n = lax.axis_size("expert")
+    depth, hid = w_gate.shape[1:]
+    lines = -(-n // 8) * 8
+    names = jnp.arange(lines, dtype=jnp.int32)[:, None]
+    comb = sum(
+        jnp.where(routes[:, k][None, :] == names, gates[:, k][None, :], 0.0) for k in range(TOP)
+    )
+    dma = pltpu.SemaphoreType.DMA
+    quarter_g, quarter_d = width // 4, hid // 4
+    outs = pl.pallas_call(
+        functools.partial(fused_kernel, n),
+        out_shape=(
+            jax.ShapeDtypeStruct((rows, width), bf16),
+            jax.ShapeDtypeStruct((quarter_g, hid), f32),
+            jax.ShapeDtypeStruct((quarter_g, hid), f32),
+            jax.ShapeDtypeStruct((quarter_d, width), f32),
+        ),
+        in_specs=[pl.BlockSpec(memory_space=pltpu.VMEM)] * 6,
+        out_specs=[pl.BlockSpec(memory_space=pltpu.VMEM)] * 4,
+        scratch_shapes=[
+            pltpu.VMEM((n, rows, width), bf16),
+            pltpu.VMEM((n, rows, width), bf16),
+            pltpu.VMEM((n, lines, rows), f32),
+            pltpu.VMEM((2, depth, hid), bf16),
+            pltpu.VMEM((2, depth, hid), bf16),
+            pltpu.VMEM((2, hid, w_down.shape[2]), bf16),
+            pltpu.VMEM((n, rows, width), bf16),
+            pltpu.VMEM((n, rows, width), bf16),
+            pltpu.VMEM((width, hid), f32),
+            pltpu.VMEM((width, hid), f32),
+            pltpu.VMEM((hid, width), f32),
+            pltpu.VMEM((2, 2, quarter_g, hid), bf16),
+            pltpu.VMEM((2, quarter_d, width), bf16),
+            pltpu.VMEM((2, 2, quarter_g, hid), bf16),
+            pltpu.VMEM((2, quarter_d, width), bf16),
+            pltpu.VMEM((2, quarter_g, hid), bf16),
+            pltpu.VMEM((quarter_d, width), bf16),
+            pltpu.VMEM((2, quarter_g, hid), bf16),
+            pltpu.VMEM((quarter_d, width), bf16),
+            dma((2, n, 3)),
+            dma((n, 3)),
+            dma((3,)),
+            dma((3,)),
+            dma((n,)),
+            dma((n,)),
+            dma((4,)),
+            dma((4,)),
+        ],
+        compiler_params=pltpu.CompilerParams(
+            collective_id=0, has_side_effects=True, vmem_limit_bytes=56 * 1024 * 1024
+        ),
+    )(tokens, upstream, comb, w_gate[0], w_up[0], w_down[0])
+    return (outs[0], outs[1][None], outs[2][None], outs[3][None])
+
+
+def per_device(*args):
+    small = lax.axis_size("expert") <= 2 * TOP and args[4].shape[0] == 1
+    if small and lax.axis_size("dp") == 2 and lax.axis_size("sub") == 2:
+        return fused(*args)
+    return routed(*args)
+
 
 def solution(mesh):
     in_specs = (

time: 208 us -> 133 us (0.64)
  waiting for transfers between devices: 128 us -> 0 us
  Pallas kernels: 0 us -> 124 us
  matrix products: 22.5 us -> 0 us
  starting transfers between devices: 13.9 us -> 0 us
  between operations: 14 us -> 0.66 us
  other arithmetic: 13.7 us -> 0.6 us
  local copies, waits for them, and re-layouts: 15 us -> 6.55 us
    pallas_call x0 -> x1, Pallas kernels: none -> 124 us  [fused(): pl.pallas_call(functools.partial(fused_kernel, n), out_shape=(jax.ShapeDt...]
    psum x1 -> x0, waiting for transfers between devices: 70.3 us -> none  [per_device(): lax.psum(part_gate.astype(jnp.bfloat16), ('dp', 'sub')).astype(jnp.float32)]
    all_to_all x3 -> x0, waiting for transfers between devices: 39.3 us -> none  [the longest x1 27.5 us: per_device(): lax.all_to_all(send_inputs, 'expert', split_axis=0, concat_axis=0, tiled=...]
    dot_general x8 -> x0, matrix products: 22.5 us -> none  [the longest x6 16 us: contract(): lax.dot_general(left, right, (((left_dim,), (right_dim,)), ((), ())), pre...]
    all_gather x3 -> x0, waiting for transfers between devices: 16.6 us -> none  [the longest x1 8.68 us: per_device(): lax.all_gather(w_up, 'sub', axis=1, tiled=True)]
    all_to_all x3 -> x0, starting transfers between devices: 13.6 us -> none  [the longest x1 6.45 us: per_device(): lax.all_to_all(send_inputs, 'expert', split_axis=0, concat_axis=0, tiled=...]
    unnamed x18 -> x14, local copies, waits for them, and re-layouts: 1.18 us -> 6.54 us
    mul x5 -> x0, local copies, waits for them, and re-layouts: 5.02 us -> none  [the longest x3 4.73 us: per_device(): gates[:, :, None] * upstream[:, None, :].astype(jnp.float32)]
  transfers between devices with their start and end apart: 7 -> 0, of which waited for: 5 -> 0; matrix products, arithmetic and copies ran while one was open for 12% -> 0% of each run, Pallas kernels for 0% -> 0%
where the time goes in v1:
time: 133 us; the launch traced here: 132 us
  Pallas kernels  124 us (93%)
  local copies, waits for them, and re-layouts  6.55 us (5%)
    pallas_call x1, Pallas kernels, fused(): pl.pallas_call(functools.partial(fused_kernel, n), out_shape=(jax.ShapeDt...  124 us
    unnamed x14, local copies, waits for them, and re-layouts  6.54 us

profile of v1, /device:TPU:0, one launch (start us, length us, event | category | flops | bytes accessed | tf_op | source)
XLA Modules:
  0.0 131.6 jit_solution(792620690371560933)
XLA Ops:
  0.6 0.0 copy-start.3
  0.6 0.7 copy-done.3
  1.3 0.0 copy-start.4
  1.3 0.7 copy-done.4
  2.0 0.6 select_add_fusion.comb_ref
  2.6 123.8 %shard_map.102 = (bf16[256,1024]{1,0:T(8,128)(2,1)}, f32[256,512]{1,0:T(8,128)}, f32[256,512]{1,0:T(8,128)}, f32[128,1024]{1,0:T(8,128)}) custom-call(bf16[256,1024]{1,0:T(8,128)(2,1)} %tok_ref.1, bf16[256,1024]{1,0:T(8,128)(2,1)} %ups_ref.1, f32[8,256]{1,0:T(8,128)} %select_add_fusion.comb_ref, bf16[512,512]{1,0:T(8,128)(2,1)} %bitcast.10, ...), custom_call_target="tpu_custom_call" | custom-call | tf_op jit(solution)/shard_map/pallas_call | solution.py:374
  126.5 0.0 copy-start.2
  126.5 1.9 %copy.15 = bf16[256,1024]{1,0:T(8,128)(2,1)} copy(bf16[256,1024]{1,0:T(8,128)(2,1)} %get-tuple-element.20) | data formatting | bytes 1048576
  128.4 0.0 copy-done.2
  128.4 0.0 copy-start.1
  128.4 0.8 copy.16
  129.2 0.4 copy-done.1
  129.6 0.0 copy-start
  129.6 0.8 copy.17
  130.4 0.4 copy-done
  130.9 0.8 copy.18
  (2 shorter events, 0.0 us)
Async XLA Ops:
  0.6 0.7 copy-start.3
  1.3 0.7 copy-start.4
  126.5 1.9 %copy-start.2 = (f32[256,512]{1,0:T(8,128)S(1)}, f32[256,512]{1,0:T(8,128)}, u32[]{:S(2)}) copy-start(f32[256,512]{1,0:T(8,128)} %get-tuple-element.9) | copy-start | bytes 1572868
  128.4 1.2 copy-start.1
  129.6 1.2 copy-start

commit v2 on v1

--- a/solution.py
+++ b/solution.py
@@ -95,6 +95,7 @@
     return (tokens_grad, slices[0][None], slices[1][None], slices[2][None])
 
 MESH = pl.DeviceIdType.MESH
+CHUNKS = 4
 
 
 def fused_kernel(
@@ -218,9 +219,17 @@
     for each in weight_waits():
         each.wait_recv()
 
-    def back_copy(block):
+    tall = back.shape[1] // CHUNKS
+
+    def back_copy(way, block, chunk):
+        rows = pl.ds(chunk * tall, tall)
+        target = jnp.minimum(z + 1, n - 1) if way == 0 else jnp.maximum(z - 1, 0)
         return copy(
-            back.at[block], landed.at[z], ig_send.at[block], ig_recv.at[z], along(block)
+            back.at[block, rows],
+            landed.at[way, block, rows],
+            ig_send.at[block, chunk],
+            ig_recv.at[way, block, chunk],
+            along(target),
         )
 
     def work(block):
@@ -245,9 +254,13 @@
                 contract(gate_grad, w_g[j], 1, 1) + contract(up_grad, w_u[j], 1, 1)
             ).astype(bf16)
 
-        @pl.when(block != z)
-        def _():
-            back_copy(block).start()
+        for way in range(2):
+            first = (z == 0) & (block > z) if way == 0 else (z == n - 1) & (block < z)
+
+            @pl.when(first)
+            def _():
+                for chunk in range(CHUNKS):
+                    back_copy(way, block, chunk).start()
 
         acc_g[...] += contract(x, gate_grad, 0, 0)
         acc_u[...] += contract(x, up_grad, 0, 0)
@@ -319,23 +332,34 @@
     gu_ref[...] = pair(acc_u, piece_g(d, s), got_gu[1, d])
     gd_ref[...] = pair(acc_d, piece_d(d, s), got_d[d])
 
-    landed[z] = back[z]
-    for source in range(n):
-
-        @pl.when(z != source)
-        def _():
-            copy(
-                back.at[source],
-                landed.at[source],
-                ig_send.at[source],
-                ig_recv.at[source],
-                along(source),
-            ).wait_recv()
-
-    total = landed[0].astype(f32)
-    for source in range(1, n):
-        total = total + landed[source].astype(f32)
-    tg_ref[...] = total.astype(bf16)
+    for key in range(1, n):
+        for chunk in range(CHUNKS):
+            rows = pl.ds(chunk * tall, tall)
+            for way in range(2):
+                block = key if way == 0 else n - 1 - key
+                relay = (z > 0) & (z < block) if way == 0 else (z < n - 1) & (z > block)
+
+                @pl.when(relay)
+                def _():
+                    hop = back_copy(way, block, chunk)
+                    hop.wait_recv()
+                    back[block, rows] = (
+                        back[block, rows].astype(f32) + landed[way, block, rows].astype(f32)
+                    ).astype(bf16)
+                    hop.start()
+
+    for chunk in range(CHUNKS):
+        rows = pl.ds(chunk * tall, tall)
+        for way in range(2):
+
+            @pl.when(z > 0 if way == 0 else z < n - 1)
+            def _():
+                back_copy(way, z, chunk).wait_recv()
+                back[z, rows] = (
+                    back[z, rows].astype(f32) + landed[way, z, rows].astype(f32)
+                ).astype(bf16)
+
+        tg_ref[rows, :] = back[z, rows]
     for each in to_dp:
         each.wait_recv()
     gg_ref[...] += in_gu[0].astype(f32)
@@ -346,9 +370,12 @@
         each.wait_send()
     for block in range(n):
 
-        @pl.when(z != block)
-        def _():
-            back_copy(block).wait_send()
+        for way in range(2):
+
+            @pl.when(z < block if way == 0 else z > block)
+            def _():
+                for chunk in range(CHUNKS):
+                    back_copy(way, block, chunk).wait_send()
 
         for way in range(2):
             mine = z >= block if way == 0 else z <= block
@@ -389,7 +416,7 @@
             pltpu.VMEM((2, depth, hid), bf16),
             pltpu.VMEM((2, hid, w_down.shape[2]), bf16),
             pltpu.VMEM((n, rows, width), bf16),
-            pltpu.VMEM((n, rows, width), bf16),
+            pltpu.VMEM((2, n, rows, width), bf16),
             pltpu.VMEM((width, hid), f32),
             pltpu.VMEM((width, hid), f32),
             pltpu.VMEM((hid, width), f32),
@@ -405,8 +432,8 @@
             dma((n, 3)),
             dma((3,)),
             dma((3,)),
-            dma((n,)),
-            dma((n,)),
+            dma((n, CHUNKS)),
+            dma((2, n, CHUNKS)),
             dma((4,)),
             dma((4,)),
         ],

time: 133 us -> 134 us (level)
    pallas_call x1, Pallas kernels: 124 us -> 125 us  [fused(): pl.pallas_call(functools.partial(fused_kernel, n), out_shape=(jax.ShapeDt...]
where the time goes in v2:
time: 134 us; the launch traced here: 133 us
  Pallas kernels  125 us (93%)
  local copies, waits for them, and re-layouts  6.55 us (5%)
    pallas_call x1, Pallas kernels, fused(): pl.pallas_call(functools.partial(fused_kernel, n), out_shape=(jax.ShapeDt...  125 us
    unnamed x14, local copies, waits for them, and re-layouts  6.54 us

profile of v2, /device:TPU:0, one launch (start us, length us, event | category | flops | bytes accessed | tf_op | source)
XLA Modules:
  0.0 133.3 jit_solution(10792155557545908575)
XLA Ops:
  0.6 0.0 copy-start.3
  0.6 0.7 copy-done.3
  1.3 0.0 copy-start.4
  1.3 0.7 copy-done.4
  2.0 0.6 select_add_fusion.comb_ref
  2.6 125.4 %shard_map.102 = (bf16[256,1024]{1,0:T(8,128)(2,1)}, f32[256,512]{1,0:T(8,128)}, f32[256,512]{1,0:T(8,128)}, f32[128,1024]{1,0:T(8,128)}) custom-call(bf16[256,1024]{1,0:T(8,128)(2,1)} %tok_ref.1, bf16[256,1024]{1,0:T(8,128)(2,1)} %ups_ref.1, f32[8,256]{1,0:T(8,128)} %select_add_fusion.comb_ref, bf16[512,512]{1,0:T(8,128)(2,1)} %bitcast.10, ...), custom_call_target="tpu_custom_call" | custom-call | tf_op jit(solution)/shard_map/pallas_call | solution.py:401
  128.1 0.0 copy-start.2
  128.1 1.9 %copy.15 = bf16[256,1024]{1,0:T(8,128)(2,1)} copy(bf16[256,1024]{1,0:T(8,128)(2,1)} %get-tuple-element.20) | data formatting | bytes 1048576
  130.0 0.0 copy-done.2
  130.0 0.0 copy-start.1
  130.0 0.8 copy.16
  130.8 0.4 copy-done.1
  131.2 0.0 copy-start
  131.2 0.8 copy.17
  132.0 0.4 copy-done
  132.5 0.8 copy.18
  (2 shorter events, 0.0 us)
Async XLA Ops:
  0.6 0.7 copy-start.3
  1.3 0.7 copy-start.4
  128.1 1.9 %copy-start.2 = (f32[256,512]{1,0:T(8,128)S(1)}, f32[256,512]{1,0:T(8,128)}, u32[]{:S(2)}) copy-start(f32[256,512]{1,0:T(8,128)} %get-tuple-element.9) | copy-start | bytes 1572868
  130.0 1.2 copy-start.1
  131.2 1.2 copy-start

commit v3 on v2

--- a/solution.py
+++ b/solution.py
@@ -96,6 +96,7 @@
 
 MESH = pl.DeviceIdType.MESH
 CHUNKS = 4
+FLIGHT = 4
 
 
 def fused_kernel(
@@ -221,8 +222,11 @@
 
     tall = back.shape[1] // CHUNKS
 
+    def chunk_rows(chunk):
+        return pl.ds(pl.multiple_of(chunk * tall, tall), tall)
+
     def back_copy(way, block, chunk):
-        rows = pl.ds(chunk * tall, tall)
+        rows = chunk_rows(chunk)
         target = jnp.minimum(z + 1, n - 1) if way == 0 else jnp.maximum(z - 1, 0)
         return copy(
             back.at[block, rows],
@@ -254,17 +258,25 @@
                 contract(gate_grad, w_g[j], 1, 1) + contract(up_grad, w_u[j], 1, 1)
             ).astype(bf16)
 
-        for way in range(2):
-            first = (z == 0) & (block > z) if way == 0 else (z == n - 1) & (block < z)
-
-            @pl.when(first)
-            def _():
-                for chunk in range(CHUNKS):
-                    back_copy(way, block, chunk).start()
-
+        def push(chunks):
+            for way in range(2):
+                first = (z == 0) & (block > z) if way == 0 else (z == n - 1) & (block < z)
+
+                @pl.when(first)
+                def _():
+                    for chunk in chunks:
+                        if chunk >= FLIGHT:
+                            back_copy(way, block, chunk - FLIGHT).wait_send()
+                        back_copy(way, block, chunk).start()
+
+        third = -(-(CHUNKS - FLIGHT) // 3)
+        push(range(FLIGHT))
         acc_g[...] += contract(x, gate_grad, 0, 0)
+        push(range(FLIGHT, min(FLIGHT + third, CHUNKS)))
         acc_u[...] += contract(x, up_grad, 0, 0)
+        push(range(FLIGHT + third, min(FLIGHT + 2 * third, CHUNKS)))
         acc_d[...] += contract(hidden, rows_grad, 0, 0)
+        push(range(FLIGHT + 2 * third, CHUNKS))
 
     def turn(i, carry):
         step, side = i // 2, i % 2
@@ -333,14 +345,15 @@
     gd_ref[...] = pair(acc_d, piece_d(d, s), got_d[d])
 
     for key in range(1, n):
-        for chunk in range(CHUNKS):
-            rows = pl.ds(chunk * tall, tall)
+        def beat(time, carry):
             for way in range(2):
                 block = key if way == 0 else n - 1 - key
+                chunk = time - z if way == 0 else time - (n - 1 - z)
                 relay = (z > 0) & (z < block) if way == 0 else (z < n - 1) & (z > block)
 
-                @pl.when(relay)
+                @pl.when(relay & (chunk >= 0) & (chunk < CHUNKS))
                 def _():
+                    rows = chunk_rows(chunk)
                     hop = back_copy(way, block, chunk)
                     hop.wait_recv()
                     back[block, rows] = (
@@ -348,6 +361,10 @@
                     ).astype(bf16)
                     hop.start()
 
+            return carry
+
+        lax.fori_loop(1, CHUNKS + n - 2, beat, 0)
+
     for chunk in range(CHUNKS):
         rows = pl.ds(chunk * tall, tall)
         for way in range(2):
@@ -374,7 +391,12 @@
 
             @pl.when(z < block if way == 0 else z > block)
             def _():
-                for chunk in range(CHUNKS):
+                for chunk in range(CHUNKS - FLIGHT, CHUNKS):
+                    back_copy(way, block, chunk).wait_send()
+
+            @pl.when((z > 0) & (z < block) if way == 0 else (z < n - 1) & (z > block))
+            def _():
+                for chunk in range(CHUNKS - FLIGHT):
                     back_copy(way, block, chunk).wait_send()
 
         for way in range(2):

time: 134 us -> 112 us (0.84)
  Pallas kernels: 125 us -> 104 us
    pallas_call x1, Pallas kernels: 125 us -> 104 us  [fused(): pl.pallas_call(functools.partial(fused_kernel, n), out_shape=(jax.ShapeDt...]
where the time goes in v3:
time: 112 us; the launch traced here: 111 us
  Pallas kernels  104 us (93%)
  local copies, waits for them, and re-layouts  6.55 us (6%)
    pallas_call x1, Pallas kernels, fused(): pl.pallas_call(functools.partial(fused_kernel, n), out_shape=(jax.ShapeDt...  104 us
    unnamed x14, local copies, waits for them, and re-layouts  6.54 us

profile of v3, /device:TPU:0, one launch (start us, length us, event | category | flops | bytes accessed | tf_op | source)
XLA Modules:
  0.0 111.5 jit_solution(16991455078093279237)
XLA Ops:
  0.6 0.0 copy-start.3
  0.6 0.7 copy-done.3
  1.3 0.0 copy-start.4
  1.3 0.7 copy-done.4
  2.0 0.6 select_add_fusion.comb_ref
  2.6 103.7 %shard_map.102 = (bf16[256,1024]{1,0:T(8,128)(2,1)}, f32[256,512]{1,0:T(8,128)}, f32[256,512]{1,0:T(8,128)}, f32[128,1024]{1,0:T(8,128)}) custom-call(bf16[256,1024]{1,0:T(8,128)(2,1)} %tok_ref.1, bf16[256,1024]{1,0:T(8,128)(2,1)} %ups_ref.1, f32[8,256]{1,0:T(8,128)} %select_add_fusion.comb_ref, bf16[512,512]{1,0:T(8,128)(2,1)} %bitcast.10, ...), custom_call_target="tpu_custom_call" | custom-call | tf_op jit(solution)/shard_map/pallas_call | solution.py:423
  106.3 0.0 copy-start.2
  106.3 1.9 %copy.15 = bf16[256,1024]{1,0:T(8,128)(2,1)} copy(bf16[256,1024]{1,0:T(8,128)(2,1)} %get-tuple-element.20) | data formatting | bytes 1048576
  108.2 0.0 copy-done.2
  108.2 0.0 copy-start.1
  108.2 0.8 copy.16
  109.0 0.4 copy-done.1
  109.5 0.0 copy-start
  109.5 0.8 copy.17
  110.3 0.4 copy-done
  110.7 0.8 copy.18
  (2 shorter events, 0.0 us)
Async XLA Ops:
  0.6 0.7 copy-start.3
  1.3 0.7 copy-start.4
  106.3 1.9 %copy-start.2 = (f32[256,512]{1,0:T(8,128)S(1)}, f32[256,512]{1,0:T(8,128)}, u32[]{:S(2)}) copy-start(f32[256,512]{1,0:T(8,128)} %get-tuple-element.9) | copy-start | bytes 1572868
  108.2 1.2 %copy-start.1 = (f32[256,512]{1,0:T(8,128)S(1)}, f32[256,512]{1,0:T(8,128)}, u32[]{:S(2)}) copy-start(f32[256,512]{1,0:T(8,128)} %get-tuple-element.10) | copy-start | bytes 1572868
  109.5 1.2 %copy-start = (f32[128,1024]{1,0:T(8,128)S(1)}, f32[128,1024]{1,0:T(8,128)}, u32[]{:S(2)}) copy-start(f32[128,1024]{1,0:T(8,128)} %get-tuple-element.11) | copy-start | bytes 1572868

commit v4 on v3

--- a/solution.py
+++ b/solution.py
@@ -101,6 +101,7 @@
 
 def fused_kernel(
     n,
+    cap,
     tok_ref,
     ups_ref,
     comb_ref,
@@ -117,6 +118,8 @@
     w_g,
     w_u,
     w_d,
+    pack_x,
+    pack_u,
     back,
     landed,
     acc_g,
@@ -154,6 +157,9 @@
     sub_peer = (group, z, d, 1 - s)
     dp_peer = (group, z, 1 - d, s)
 
+    tail = (n, x_all.shape[1] - cap, x_all.shape[2])
+    x_all[:, cap:, :] = jnp.zeros(tail, bf16)
+    u_all[:, cap:, :] = jnp.zeros(tail, bf16)
     barrier = pltpu.get_barrier_semaphore()
     for step in range(1, n):
         pl.semaphore_signal(
@@ -179,26 +185,57 @@
             device_id_type=MESH,
         )
 
-    def block_copies(way, block):
+    size = x_all.shape[1]
+
+    def placing(block, expert, compact):
+        comb = c_all[block]
+        before = lax.broadcasted_iota(jnp.int32, (size, size), 0)
+        after = lax.broadcasted_iota(jnp.int32, (size, size), 1)
+        upper = jnp.where(before <= after, 1.0, 0.0).astype(bf16)
+        count = contract(jnp.where(comb > 0.0, 1.0, 0.0).astype(bf16), upper, 1, 0)
+        line = lax.broadcasted_iota(jnp.int32, comb.shape, 0)
+        weight = jnp.sum(jnp.where(line == expert, comb, 0.0), axis=0, keepdims=True)
+        count = jnp.sum(jnp.where(line == expert, count, 0.0), axis=0, keepdims=True)
+        place = compact * (count - 1.0) + (1.0 - compact) * after[:1].astype(f32)
+        hit = (before.astype(f32) == place) & (weight > 0.0)
+        column = jnp.sum(jnp.where(hit, weight, 0.0), axis=1, keepdims=True)
+        return jnp.where(hit, 1.0, 0.0).astype(bf16), column
+
+    def block_copies(way, block, packed):
         target = jnp.minimum(z + 1, n - 1) if way == 0 else jnp.maximum(z - 1, 0)
+        refs = [(c_all.at[block], c_all.at[block])]
+        for pack, ref in ((pack_u, u_all), (pack_x, x_all)):
+            if packed:
+                refs.append((pack.at[way, block], ref.at[block, pl.ds(0, cap)]))
+            else:
+                refs.append((ref.at[block], ref.at[block]))
         return [
-            copy(
-                ref.at[block],
-                ref.at[block],
-                ag_send.at[way, block, i],
-                ag_recv.at[block, i],
-                along(target),
-            )
-            for i, ref in enumerate((c_all, u_all, x_all))
+            copy(src, dst, ag_send.at[way, block, i], ag_recv.at[block, i], along(target))
+            for i, (src, dst) in enumerate(refs)
         ]
 
     can_go = (z < n - 1, z > 0)
+    to_end = (z == n - 2, z == 1)
+    at_end = (z == n - 1, z == 0)
+
+    def send_block(way, block, allowed):
+        @pl.when(allowed & jnp.logical_not(to_end[way]))
+        def _():
+            for each in block_copies(way, block, False):
+                each.start()
+
+        @pl.when(allowed & to_end[way])
+        def _():
+            one_hot = placing(block, n - 1 if way == 0 else 0, 1.0)[0][:cap]
+            copies = block_copies(way, block, True)
+            copies[0].start()
+            pack_u[way, block] = contract(one_hot, u_all[block], 1, 0).astype(bf16)
+            copies[1].start()
+            pack_x[way, block] = contract(one_hot, x_all[block], 1, 0).astype(bf16)
+            copies[2].start()
+
     for way in range(2):
-
-        @pl.when(can_go[way])
-        def _():
-            for each in block_copies(way, z):
-                each.start()
+        send_block(way, z, can_go[way])
 
     def weight_copies():
         return [
@@ -238,9 +275,8 @@
 
     def work(block):
         x = x_all[block]
-        flipped = jnp.transpose(c_all[block])
-        lane = lax.broadcasted_iota(jnp.int32, flipped.shape, 1)
-        weight = jnp.sum(jnp.where(lane == z, flipped, 0.0), axis=1, keepdims=True)
+        ends = (z == 0) | (z == n - 1)
+        one_hot, weight = placing(block, z, jnp.where(ends & (block != z), 1.0, 0.0))
         rows_grad = (weight * u_all[block].astype(f32)).astype(bf16)
         x_lo, x_hi = x[:, :half], x[:, half:]
         gate_pre = contract(x_lo, w_g[0], 1, 0) + contract(x_hi, w_g[1], 1, 0)
@@ -254,8 +290,9 @@
         gate_grad = (hidden_grad * up_pre * sig * (1.0 + gate_pre * (1.0 - sig))).astype(bf16)
         up_grad = (hidden_grad * silu).astype(bf16)
         for j in range(2):
-            back[block, :, j * half : (j + 1) * half] = (
-                contract(gate_grad, w_g[j], 1, 1) + contract(up_grad, w_u[j], 1, 1)
+            part = contract(gate_grad, w_g[j], 1, 1) + contract(up_grad, w_u[j], 1, 1)
+            back[block, :, j * half : (j + 1) * half] = contract(
+                one_hot, part.astype(bf16), 0, 0
             ).astype(bf16)
 
         def push(chunks):
@@ -287,15 +324,15 @@
                 block = z - step if way == 0 else z + step
                 there = block >= 0 if way == 0 else block < n
 
-                @pl.when(there)
-                def _():
-                    for each in block_copies(way, block):
-                        each.wait_recv()
-
-                @pl.when(there & can_go[way])
-                def _():
-                    for each in block_copies(way, block):
-                        each.start()
+                for packed in range(2):
+                    form = at_end[way] if packed else jnp.logical_not(at_end[way])
+
+                    @pl.when(there & form)
+                    def _():
+                        for each in block_copies(way, block, packed):
+                            each.wait_recv()
+
+                send_block(way, block, there & can_go[way])
 
         block = z - step + 2 * step * side
 
@@ -402,10 +439,13 @@
         for way in range(2):
             mine = z >= block if way == 0 else z <= block
 
-            @pl.when(mine & can_go[way])
-            def _():
-                for each in block_copies(way, block):
-                    each.wait_send()
+            for packed in range(2):
+                form = to_end[way] if packed else jnp.logical_not(to_end[way])
+
+                @pl.when(mine & can_go[way] & form)
+                def _():
+                    for each in block_copies(way, block, packed):
+                        each.wait_send()
 
 
 def fused(tokens, upstream, routes, gates, w_gate, w_up, w_down):
@@ -414,6 +454,7 @@
     n = lax.axis_size("expert")
     depth, hid = w_gate.shape[1:]
     lines = -(-n // 8) * 8
+    cap = min(rows, 3 * rows * TOP // (2 * n))
     names = jnp.arange(lines, dtype=jnp.int32)[:, None]
     comb = sum(
         jnp.where(routes[:, k][None, :] == names, gates[:, k][None, :], 0.0) for k in range(TOP)
@@ -421,7 +462,7 @@
     dma = pltpu.SemaphoreType.DMA
     quarter_g, quarter_d = width // 4, hid // 4
     outs = pl.pallas_call(
-        functools.partial(fused_kernel, n),
+        functools.partial(fused_kernel, n, cap),
         out_shape=(
             jax.ShapeDtypeStruct((rows, width), bf16),
             jax.ShapeDtypeStruct((quarter_g, hid), f32),
@@ -437,6 +478,8 @@
             pltpu.VMEM((2, depth, hid), bf16),
             pltpu.VMEM((2, depth, hid), bf16),
             pltpu.VMEM((2, hid, w_down.shape[2]), bf16),
+            pltpu.VMEM((2, n, cap, width), bf16),
+            pltpu.VMEM((2, n, cap, width), bf16),
             pltpu.VMEM((n, rows, width), bf16),
             pltpu.VMEM((2, n, rows, width), bf16),
             pltpu.VMEM((width, hid), f32),

time: 112 us -> 106 us (0.946)
  Pallas kernels: 104 us -> 98.2 us
    pallas_call x1, Pallas kernels: 104 us -> 98.2 us  [fused(): pl.pallas_call(functools.partial(fused_kernel, n, cap), out_shape=(jax.Sh...]
where the time goes in v4:
time: 106 us
  Pallas kernels  98.2 us (93%)
  local copies, waits for them, and re-layouts  6.55 us (6%)
    pallas_call x1, Pallas kernels, fused(): pl.pallas_call(functools.partial(fused_kernel, n, cap), out_shape=(jax.Sh...  98.2 us
    unnamed x14, local copies, waits for them, and re-layouts  6.54 us

profile of v4, /device:TPU:0, one launch (start us, length us, event | category | flops | bytes accessed | tf_op | source)
XLA Modules:
  0.0 106.1 jit_solution(14118948145084000498)
XLA Ops:
  0.6 0.0 copy-start.3
  0.6 0.7 copy-done.3
  1.3 0.0 copy-start.4
  1.3 0.7 copy-done.4
  2.0 0.6 select_add_fusion.comb_ref
  2.6 98.2 %shard_map.102 = (bf16[256,1024]{1,0:T(8,128)(2,1)}, f32[256,512]{1,0:T(8,128)}, f32[256,512]{1,0:T(8,128)}, f32[128,1024]{1,0:T(8,128)}) custom-call(bf16[256,1024]{1,0:T(8,128)(2,1)} %tok_ref.1, bf16[256,1024]{1,0:T(8,128)(2,1)} %ups_ref.1, f32[8,256]{1,0:T(8,128)} %select_add_fusion.comb_ref, bf16[512,512]{1,0:T(8,128)(2,1)} %bitcast.10, ...), custom_call_target="tpu_custom_call" | custom-call | tf_op jit(solution)/shard_map/pallas_call | solution.py:464
  100.9 0.0 copy-start.2
  100.9 1.9 %copy.15 = bf16[256,1024]{1,0:T(8,128)(2,1)} copy(bf16[256,1024]{1,0:T(8,128)(2,1)} %get-tuple-element.20) | data formatting | bytes 1048576
  102.8 0.0 copy-done.2
  102.8 0.0 copy-start.1
  102.8 0.8 copy.16
  103.6 0.4 copy-done.1
  104.0 0.0 copy-start
  104.0 0.8 copy.17
  104.8 0.4 copy-done
  105.3 0.8 copy.18
  (2 shorter events, 0.0 us)
Async XLA Ops:
  0.6 0.7 copy-start.3
  1.3 0.7 copy-start.4
  100.9 1.9 %copy-start.2 = (f32[256,512]{1,0:T(8,128)S(1)}, f32[256,512]{1,0:T(8,128)}, u32[]{:S(2)}) copy-start(f32[256,512]{1,0:T(8,128)} %get-tuple-element.9) | copy-start | bytes 1572868
  102.8 1.2 %copy-start.1 = (f32[256,512]{1,0:T(8,128)S(1)}, f32[256,512]{1,0:T(8,128)}, u32[]{:S(2)}) copy-start(f32[256,512]{1,0:T(8,128)} %get-tuple-element.10) | copy-start | bytes 1572868
  104.0 1.2 %copy-start = (f32[128,1024]{1,0:T(8,128)S(1)}, f32[128,1024]{1,0:T(8,128)}, u32[]{:S(2)}) copy-start(f32[128,1024]{1,0:T(8,128)} %get-tuple-element.11) | copy-start | bytes 1572868
